TPU v7x, 128 devices: a whole 4x4x4 slice. The times are simulated.
128 devices in a mesh: child: 4 (over z_hi, core), col: 32 (over y, x, z_lo).
Axes of the slice: x: 4, y: 4, z: 4 (z_hi: 2, z_lo: 2; z = z_hi * 2 + z_lo), core: 2. Of those that a mesh axis runs over, the one named last changes fastest.
Arguments:
- parent_entries: float32 [16384, 16384], P('child', 'col'), as said below
- updates: float32 [4, 8192, 8192], P('child', 'col'), as said below
- block_maps: int32 [4, 64], replicated, may hold values from 0 to 127, as said below
- live_blocks: int32 [4, 64], replicated, may hold values 0 or 1
Outputs:
- factored: float32 [16384, 16384], P('child', 'col')
Inputs may be any that keep to these rules, and one draw needn't show every extreme that they name: For every sibling c and block t, block_maps[c, t] // 4 == t // 2, and each sibling's row is strictly increasing: a sibling covers two of every four aligned parent blocks, and half of the parent's blocks in all. `parent_entries`: Symmetric, with diagonal entries between 1 and 2; the assembled parent is positive definite. `updates`: each sibling's matrix is symmetric.
All inputs are finite; a program needn't handle non-finite values.
Results may differ from a plain program's by a relative error of at most 0.0001.
Values sent between devices are 32-bit elements; how exact they have to be, the bound alone decides.
A program may use at most 192 MiB of HBM per device.

v0:
```python
import jax
import jax.numpy as jnp
from jax import lax
from jax.sharding import PartitionSpec as P

BLOCK = 128
PANELS = 2


HIGHEST = lax.Precision.HIGHEST


def spread(block, axis, source):
    block = jnp.where(lax.axis_index(axis) == source, block, jnp.zeros_like(block))
    return lax.psum(block, axis)


def inverse_factor(block):
    lower_part = jnp.linalg.cholesky(block)
    identity = jnp.eye(block.shape[0], dtype=block.dtype)
    return lax.linalg.triangular_solve(lower_part, identity, left_side=True, lower=True)


def per_device(parent_entries, updates, block_maps, live_blocks):
    row_group = lax.axis_index("child")
    col_group = lax.axis_index("col")
    groups = lax.axis_size("child")
    owners = lax.axis_size("col")
    local_rows, panel_width = parent_entries.shape
    child_order = updates.shape[2]
    by_owner = lax.all_to_all(
        lax.all_to_all(updates[0], "col", split_axis=1, concat_axis=0, tiled=True),
        "child",
        split_axis=0,
        concat_axis=0,
        tiled=True,
    )
    tile_count = child_order // BLOCK // groups
    pair_count = child_order // BLOCK // owners
    gathered = by_owner.reshape(groups, tile_count, BLOCK, pair_count, BLOCK)
    alive_blocks = live_blocks.astype(jnp.float32)
    row_maps = lax.dynamic_slice_in_dim(
        block_maps, row_group * tile_count, tile_count, 1
    ) - row_group * (local_rows // BLOCK)
    row_alive = lax.dynamic_slice_in_dim(alive_blocks, row_group * tile_count, tile_count, 1)
    row_select = (row_maps[:, None, :] == jnp.arange(local_rows // BLOCK)[None, :, None]).astype(
        jnp.float32
    ) * row_alive[:, None, :]
    col_maps = lax.dynamic_slice_in_dim(
        block_maps, col_group * pair_count, pair_count, 1
    ) - col_group * (panel_width // BLOCK)
    col_alive = lax.dynamic_slice_in_dim(alive_blocks, col_group * pair_count, pair_count, 1)
    col_select = (col_maps[:, None, :] == jnp.arange(panel_width // BLOCK)[None, :, None]).astype(
        jnp.float32
    ) * col_alive[:, None, :]
    placed = jnp.einsum("cpt,ctasb->cpasb", row_select, gathered, precision=HIGHEST)
    placed = jnp.einsum("cpasb,cqs->paqb", placed, col_select, precision=HIGHEST)
    matrix = parent_entries + placed.reshape(local_rows, panel_width)
    global_rows = row_group * local_rows + jnp.arange(local_rows)
    global_cols = col_group * panel_width + jnp.arange(panel_width)
    for panel_index in range(PANELS):
        start_col = panel_index * panel_width
        stop_col = start_col + panel_width
        lower_mask = (
            global_rows[:, None] >= (start_col + jnp.arange(panel_width))[None, :]
        ).astype(jnp.float32)
        row_keep = (global_rows >= stop_col).astype(jnp.float32)[:, None]
        col_keep = (global_cols >= stop_col).astype(jnp.float32)
        column = spread(matrix, "col", panel_index)
        pivots = spread(
            jnp.stack([column[start_col:stop_col], matrix[start_col:stop_col]]), "child", 0
        )
        inverse_t = inverse_factor(pivots[0]).T
        factor = jnp.dot(column, inverse_t, precision=HIGHEST) * lower_mask
        side_rows = jnp.dot(pivots[1].T, inverse_t, precision=HIGHEST) * col_keep[:, None]
        matrix = matrix - jnp.dot(factor * row_keep, side_rows.T, precision=HIGHEST)
        matrix = jnp.where(col_group == panel_index, factor, matrix)
        zero_band = ((global_rows >= start_col) & (global_rows < stop_col))[:, None] & (
            global_cols >= stop_col
        )[None, :]
        matrix = jnp.where(zero_band, 0.0, matrix)
    return matrix


def solution(mesh):
    in_specs = (P("child", "col"), P("child", "col", None), P(), P())
    out_specs = P("child", "col")
    return jax.shard_map(
        per_device, mesh=mesh, in_specs=in_specs, out_specs=out_specs, check_vma=False
    )
```

profile of v0, /device:TPU:37, one launch (start us, length us, event | category | flops | bytes accessed | tf_op | source)
XLA Modules:
  0.0 1573.9 jit_solution(9585655397723370086)
XLA Ops:
  6.5 9.0 copy.43
  15.5 101.2 %all_to_all.25 = f32[256,32,256]{0,2,1:T(8,128)} all-to-all(f32[256,32,256]{0,2,1:T(8,128)} %bitcast.146), channel_id=1, replica_groups=mesh['child'=4,'col'=32] {'col'}, dimensions={1} | all-to-all | bytes 16777216 | tf_op jit(solution)/shard_map/all_to_all | solution.py:32
  116.8 8.9 copy.44
  125.7 7.1 all-to-all-start.1
  133.2 8.9 copy.49
  142.2 84.4 %all-to-all-done.1 = f32[4,2048,256]{2,1,0:T(8,128)} async-done(((f32[4,2048,256]{2,1,0:T(8,128)}), f32[4,2048,256]{2,1,0:T(8,128)}, u32[]{:S(2)}, u32[]{:S(2)}) %all-to-all-start.1) | async-done | bytes 8388640 | tf_op jit(solution)/shard_map/all_to_all | solution.py:31
  226.7 10.8 reshape.135
  237.5 16.4 %fusion.2 = f32[4,32,128,2,128]{4,1,3,2,0:T(8,128)S(1)} fusion(f32[4,16,128,2,128]{4,3,2,1,0:T(2,128)} %reshape.135, f32[4,16]{1,0:T(4,128)S(1)} %constant_dynamic-slice_fusion.2, s32[4,16]{1,0:T(4,128)S(1)} %dynamic-slice_subtract_fusion), kind=kOutput, calls=%fused_computation.7 | convolution fusion | flops 805310464 | bytes 25166336 | tf_op jit(solution)/shard_map/cpt,ctasb->cpasb/dot_general | solution.py:56
  253.9 39.3 %fusion = f32[4,32,128,128,1]{3,0,4,2,1:T(4,128)S(1)} fusion(f32[4,32,128,2,128]{4,1,3,2,0:T(8,128)S(1)} %fusion.2, f32[4,2]{0,1:T(2,128)S(1)} %copy.42, s32[4,2]{0,1:T(2,128)S(1)} %copy.41), kind=kOutput, calls=%fused_computation.4 | convolution fusion | flops 201326656 | bytes 25165888 | tf_op jit(solution)/shard_map/cpasb,cqs->paqb/dot_general | solution.py:57
  293.2 4.2 copy.73
  297.4 8.9 copy.66
  306.3 10.8 broadcast_select_fusion.1
  318.5 371.2 %all-reduce.6.cloned.1.call-done = f32[4096,512]{0,1:T(8,128)} async-done(((f32[4096,512]{0,1:T(8,128)}), f32[4096,512]{0,1:T(8,128)}) %all-reduce.6.cloned.1.call-update) | async-done | bytes 8388624 | tf_op jit(solution)/shard_map/psum | solution.py:15
  691.0 1.5 maximum_select_fusion
  693.2 60.5 %all-reduce.8.cloned.1.call-done = f32[2,512,512]{1,2,0:T(8,128)} async-done(((f32[2,512,512]{1,2,0:T(8,128)}), f32[2,512,512]{1,2,0:T(8,128)}) %all-reduce.8.cloned.1.call-update) | async-done | bytes 2097168 | tf_op jit(solution)/shard_map/psum | solution.py:15
  755.3 1.4 fusion.22
  756.8 11.7 cholesky.286
  768.7 9.8 custom-call.27
  779.2 11.7 cholesky.305
  790.9 9.9 custom-call.28
  801.5 11.7 cholesky.326
  813.9 9.8 custom-call.29
  824.3 11.7 cholesky.343
  840.3 7.9 while.4
  840.9 1.4 bitcast_dynamic-update-slice_fusion.4
  842.9 1.4 bitcast_dynamic-update-slice_fusion.4
  844.9 1.4 bitcast_dynamic-update-slice_fusion.4
  848.2 39.3 %custom-call.30 = f32[4,128,128]{1,2,0:T(8,128)S(1)} custom-call(f32[4,128,128]{2,1,0:T(8,128)S(1)} %get-tuple-element.21), custom_call_target="InvertDiagBlocksLowerTriangular" | custom-call | tf_op jit(solution)/shard_map/triangular_solve/custom-call.3 | solution.py:21
  890.7 17.3 %fusion.35 = f32[4096,512]{0,1:T(8,128)} fusion(f32[4096,512]{0,1:T(8,128)} %all-reduce.6.cloned.1.call-done, f32[128,512]{1,0:T(8,128)S(1)} %fusion.68, f32[128,512]{1,0:T(8,128)S(1)} %fusion.69, f32[128,512]{1,0:T(8,128)S(1)} %fusion.71, f32[128,512]{1,0:T(8,128)S(1)} %fusion.46), kind=kOutput, calls=%fused_computation.77 | convolution fusion | flops 12885688320 | bytes 17825792 | tf_op jit(solution)/shard_map/dot_general | solution.py:74
  908.0 1.9 convolution_multiply_fusion.1
  909.9 33.7 %broadcast_select_fusion = (f32[4096,512]{0,1:T(8,128)}, f32[4096,512]{0,1:T(8,128)}) fusion(pred[]{:T(512)S(6)} %eq.44, f32[4096,512]{0,1:T(8,128)} %get-tuple-element.40, f32[512,512]{1,0:T(8,128)S(1)} %convolution_multiply_fusion.1, f32[4096,512]{0,1:T(8,128)} %fusion.35, f32[4096]{0:T(1024)S(1)} %get-tuple-element.75, s32[4096]{0:T(1024)S(1)} %iota_add_fusion, ...), kind=kOutput, calls=%fused_computation.22 | convolution fusion | flops 12905873408 | bytes 34640384 | tf_op jit(solution)/shard_map/dot_general | solution.py:76
  945.2 371.7 %all-reduce.10.cloned.1.call-done = f32[4096,512]{0,1:T(8,128)} async-done(((f32[4096,512]{0,1:T(8,128)}), f32[4096,512]{0,1:T(8,128)}) %all-reduce.10.cloned.1.call-update) | async-done | bytes 8388624 | tf_op jit(solution)/shard_map/psum | solution.py:15
  1318.1 1.5 maximum_select_fusion.1
  1319.8 61.0 %all-reduce.12.cloned.1.call-done = f32[2,512,512]{1,2,0:T(8,128)} async-done(((f32[2,512,512]{1,2,0:T(8,128)}), f32[2,512,512]{1,2,0:T(8,128)}) %all-reduce.12.cloned.1.call-update) | async-done | bytes 2097168 | tf_op jit(solution)/shard_map/psum | solution.py:15
  1382.4 1.4 fusion.21
  1383.9 11.7 cholesky.358
  1395.8 9.8 custom-call.31
  1406.3 11.7 cholesky.377
  1419.3 10.2 custom-call.32
  1430.2 11.7 cholesky.398
  1442.6 9.8 custom-call.33
  1453.0 11.9 cholesky.415
  1468.1 8.0 while.5
  1476.1 39.3 %custom-call.34 = f32[4,128,128]{1,2,0:T(8,128)S(1)} custom-call(f32[4,128,128]{2,1,0:T(8,128)S(1)} %get-tuple-element.22), custom_call_target="InvertDiagBlocksLowerTriangular" | custom-call | tf_op jit(solution)/shard_map/triangular_solve/custom-call.3 | solution.py:21
  1518.6 17.7 %fusion.34 = f32[4096,512]{0,1:T(8,128)S(1)} fusion(f32[4096,512]{0,1:T(8,128)} %all-reduce.10.cloned.1.call-done, f32[128,512]{1,0:T(8,128)S(1)} %fusion.62, f32[128,512]{1,0:T(8,128)S(1)} %fusion.63, f32[128,512]{1,0:T(8,128)S(1)} %fusion.65, f32[128,512]{1,0:T(8,128)S(1)} %fusion.44), kind=kOutput, calls=%fused_computation.76 | convolution fusion | flops 12885688320 | bytes 17825792 | tf_op jit(solution)/shard_map/dot_general | solution.py:74
  1536.3 1.9 convolution_multiply_fusion
  1538.2 20.0 %select_select_fusion = f32[4096,512]{0,1:T(8,128)} fusion(f32[4096,512]{0,1:T(8,128)} %get-tuple-element.68, f32[4096,512]{0,1:T(8,128)S(1)} %fusion.34, f32[512,512]{1,0:T(8,128)S(1)} %convolution_multiply_fusion, f32[4096]{0:T(1024)S(1)} %get-tuple-element.78, s32[4096]{0:T(1024)S(1)} %iota_add_fusion, s32[512]{0:T(512)S(1)} %iota_add_fusion.1, ...), kind=kOutput, calls=%fused_computation.9 | convolution fusion | flops 12903776256 | bytes 26253824 | tf_op jit(solution)/shard_map/dot_general | solution.py:76
  1558.2 8.9 copy.56
  (115 shorter events, 37.2 us)
Async XLA Ops:
  125.7 7.1 copy-start.3
  125.7 7.2 copy-start.2
  125.7 101.0 %all-to-all-start.1 = ((f32[4,2048,256]{2,1,0:T(8,128)}), f32[4,2048,256]{2,1,0:T(8,128)}, u32[]{:S(2)}, u32[]{:S(2)}) async-start(f32[4,2048,256]{2,1,0:T(8,128)} %bitcast.143), calls=%async_computation.1 | async-start | bytes 16777216 | tf_op jit(solution)/shard_map/all_to_all | solution.py:31
  132.8 556.9 %all-reduce.6.cloned.1.call-start = ((), (), s32[]{:S(2)}) async-start(), calls=%async_computation.2 | async-start | bytes 16777216 | tf_op jit(solution)/shard_map/psum | solution.py:15
  317.2 436.5 %all-reduce.8.cloned.1.call-start = ((), (), s32[]{:S(2)}) async-start(), calls=%async_computation.3 | async-start | bytes 4194304 | tf_op jit(solution)/shard_map/psum | solution.py:15
  692.6 624.2 %all-reduce.10.cloned.1.call-start = ((), (), s32[]{:S(2)}) async-start(), calls=%async_computation.4 | async-start | bytes 16777216 | tf_op jit(solution)/shard_map/psum | solution.py:15
  890.7 17.3 %copy-start = (f32[2,512,512]{1,2,0:T(8,128)S(1)}, f32[2,512,512]{1,2,0:T(8,128)}, u32[]{:S(2)}) copy-start(f32[2,512,512]{1,2,0:T(8,128)} %all-reduce.8.cloned.1.call-done) | copy-start | bytes 6291460
  943.6 437.2 %all-reduce.12.cloned.1.call-start = ((), (), s32[]{:S(2)}) async-start(), calls=%async_computation.5 | async-start | bytes 4194304 | tf_op jit(solution)/shard_map/psum | solution.py:15
  1518.6 17.7 %copy-start.1 = (f32[2,512,512]{1,2,0:T(8,128)S(1)}, f32[2,512,512]{1,2,0:T(8,128)}, u32[]{:S(2)}) copy-start(f32[2,512,512]{1,2,0:T(8,128)} %all-reduce.12.cloned.1.call-done) | copy-start | bytes 6291460
Sparse Core Ops, SparseCore 0:
  317.3 372.3 all-reduce.5
  692.7 60.9 all-reduce.7
  943.8 373.0 all-reduce.9
  1319.8 60.9 all-reduce.11
where the time goes:
time: 1580 us; the launch traced here: 1570 us
  waiting for transfers between devices  949 us (60%)
  other arithmetic  254 us (16%)
  matrix products  158 us (10%)
  blocking collectives  101 us (6%)
  local copies, waits for them, and re-layouts  84.5 us (5%)
  between operations  18.8 us (1%)
    psum x4, waiting for transfers between devices, spread(): return lax.psum(block, axis)  864 us
    another operation x29, other arithmetic, inverse_factor(): lower_part = jnp.linalg.cholesky(block)  158 us
    all_to_all x1, blocking collectives, per_device(): lax.all_to_all(updates[0], 'col', split_axis=1, concat_axis=0, tiled=True)  101 us
    all_to_all x1, waiting for transfers between devices, per_device(): lax.all_to_all(lax.all_to_all(updates[0], 'col', split_axis=1, concat_axi...  84.4 us
    another operation x5, other arithmetic, inverse_factor(): lax.linalg.triangular_solve(lower_part, identity, left_side=True, lower=T...  78.9 us
    dot_general x2, matrix products, per_device(): matrix = matrix - jnp.dot(factor * row_keep, side_rows.T, precision=HIGHEST)  53.7 us
    dot_general x1, matrix products, per_device(): jnp.einsum('cpasb,cqs->paqb', placed, col_select, precision=HIGHEST)  39.3 us
    dot_general x2, matrix products, per_device(): factor = jnp.dot(column, inverse_t, precision=HIGHEST) * lower_mask  35 us
  transfers between devices with their start and end apart: 5, of which 5 were waited for; matrix products, arithmetic and copies ran while one was open for 1% of the time, Pallas kernels for 0%

commit v1 on v0

v1 whole, which is shorter than its diff:
```python
import functools

import jax
import jax.numpy as jnp
from jax import lax
from jax.experimental import pallas as pl
from jax.experimental.pallas import tpu as pltpu
from jax.sharding import PartitionSpec as P

HIGHEST = lax.Precision.HIGHEST


def recip(d):
    r = pl.reciprocal(d, approx=True)
    r = r*(2.0-d*r)
    return r*(2.0-d*r)
def rsq(d):
    r = lax.rsqrt(d)
    return r*(1.5-0.5*d*r*r)
def diag_inverse(tile):
    rows=[tile[8*g:8*g+8,:] for g in range(16)]
    lane=lax.broadcasted_iota(jnp.int32,(8,128),1)
    sub=lax.broadcasted_iota(jnp.int32,(8,128),0)
    wide=lambda v: jnp.broadcast_to(v,(8,128))
    for m in range(16):
        o=8*m
        V=rows[m]
        b={(i,q): wide(V[i:i+1,o+q:o+q+1]) for i in range(8) for q in range(i+1)}
        cols={(g,q): wide(rows[g][:,o+q:o+q+1]) for g in range(m+1,16) for q in range(8)}
        inside=(lane>=o)&(lane<o+8)
        V=jnp.where(inside, jnp.where(lane-o==sub,1.0,0.0), V)
        v=[wide(V[i:i+1,:]) for i in range(8)]
        l={}; rd=[]
        for q in range(8):
            rd.append(recip(b[q,q]))
            for i in range(q+1,8):
                l[i,q]=b[i,q]*rd[q]
                for c in range(q+1,i+1):
                    b[i,c]=b[i,c]-l[i,q]*b[c,q]
                v[i]=v[i]-l[i,q]*v[q]
        t=[v[i]*rd[i] for i in range(8)]
        for i in range(6,-1,-1):
            for c in range(i+1,8):
                t[i]=t[i]-l[c,i]*t[c]
        new=v[0]*rsq(b[0,0])
        for i in range(1,8):
            new=jnp.where(sub==i, v[i]*rsq(b[i,i]), new)
        rows[m]=new
        for g in range(m+1,16):
            acc=jnp.where(inside,0.0,rows[g])
            for q in range(8):
                acc=acc-cols[g,q]*t[q]
            rows[g]=acc
    full=jnp.concatenate(rows,0)
    r=lax.broadcasted_iota(jnp.int32,(128,128),0); c=lax.broadcasted_iota(jnp.int32,(128,128),1)
    return jnp.where(c<=r, full, 0.0)
def factor_step(S, k):
    at=pl.ds(pl.multiple_of(k*128,128),128)
    inv=diag_inverse(S[at,at])
    r=lax.broadcasted_iota(jnp.int32,(128,128),0); c=lax.broadcasted_iota(jnp.int32,(128,128),1)
    S[at,at]=jnp.where(r==c,1.0,0.0)
    S[at,:]=jnp.dot(inv,S[at,:],precision=HIGHEST,preferred_element_type=jnp.float32)
    def body(i,_):
        ri=pl.ds(pl.multiple_of(i*128,128),128)
        L=S[at,ri]
        S[ri,at]=jnp.zeros((128,128),jnp.float32)
        S[ri,:]=S[ri,:]-lax.dot_general(L,S[at,:],(((0,),(0,)),((),())),precision=HIGHEST,preferred_element_type=jnp.float32)
        return 0
    lax.fori_loop(k+1,8,body,0)


def finish_body(place_ref, map_ref, live_ref, parent_ref, upd_ref, panel_ref, wt_ref, out_ref, whi, wlo, acc):
    i=pl.program_id(0)
    r=place_ref[0]; j=place_ref[1]
    @pl.when(i==0)
    def _():
        w=wt_ref[...]
        h=w.astype(jnp.bfloat16)
        whi[...]=h
        wlo[...]=(w-h.astype(jnp.float32)).astype(jnp.bfloat16)
    a=panel_ref[0]
    ahi=a.astype(jnp.bfloat16)
    alo=(a-ahi.astype(jnp.float32)).astype(jnp.bfloat16)
    dot=lambda x,y: jnp.dot(x,y,preferred_element_type=jnp.float32)
    acc[...]=dot(whi[...],ahi)+(dot(whi[...],alo)+dot(wlo[...],ahi))
    keep=jnp.where(j>=2,1.0,0.0).astype(jnp.float32)
    for c in range(4):
        for q in range(2):
            col=2*j+q
            bq=map_ref[c,col]-4*j
            lq=live_ref[c,col].astype(jnp.float32)*keep
            for p in range(2):
                row=16*r+2*i+p
                ap=map_ref[c,row]-4*(8*r+i)
                w=lq*live_ref[c,row].astype(jnp.float32)
                dst=(pl.ds(pl.multiple_of(bq*128,128),128),pl.ds(pl.multiple_of(ap*128,128),128))
                acc[dst]=acc[dst]+w*upd_ref[c,q*128:q*128+128,p*128:p*128+128]
    total=acc[...].T+keep*parent_ref[...]
    g=r*4096+i*512+lax.broadcasted_iota(jnp.int32,(512,512),0)
    s=j*512+lax.broadcasted_iota(jnp.int32,(512,512),1)
    out_ref[...]=jnp.where(g<jnp.minimum(s,1024),0.0,total)
def finish(place,maps,live,parent,upd,panel,wt):
    spec=pltpu.PrefetchScalarGridSpec(num_scalar_prefetch=3,grid=(8,),
      in_specs=[pl.BlockSpec((512,512),lambda i,*_:(i,0)),
                pl.BlockSpec((4,256,256),lambda i,*_:(0,0,i)),
                pl.BlockSpec((1,1024,512),lambda i,*_:(i,0,0)),
                pl.BlockSpec((512,1024),lambda i,*_:(0,0))],
      out_specs=pl.BlockSpec((512,512),lambda i,*_:(i,0)),
      scratch_shapes=[pltpu.VMEM((512,1024),jnp.bfloat16),pltpu.VMEM((512,1024),jnp.bfloat16),pltpu.VMEM((512,512),jnp.float32)])
    return pl.pallas_call(finish_body,grid_spec=spec,out_shape=jax.ShapeDtypeStruct((4096,512),jnp.float32),
      compiler_params=pltpu.CompilerParams(vmem_limit_bytes=48*2**20),
      cost_estimate=pl.CostEstimate(flops=3*2*4096*512*1024,bytes_accessed=45*2**20,transcendentals=0))(place,maps,live,parent,upd,panel,wt)


MESH = pl.DeviceIdType.MESH


class Links:
    def __init__(self, send_sem, recv_sem):
        self.send_sem, self.recv_sem, self.used = send_sem, recv_sem, 0
        self.pending = []

    def slot(self):
        self.used += 1
        return self.used - 1

    def copy(self, slot, source, target, device):
        return pltpu.make_async_remote_copy(
            src_ref=source,
            dst_ref=target,
            send_sem=self.send_sem.at[slot],
            recv_sem=self.recv_sem.at[slot],
            device_id=device,
            device_id_type=MESH,
        )

    def send(self, slot, ends):
        self.copy(slot, *ends()).start()
        self.pending.append((slot, ends))

    def landed(self, slot, region, device):
        self.copy(slot, region, region, device).wait_recv()

    def drain(self):
        for slot, ends in self.pending:
            self.copy(slot, *ends()).wait_send()
        self.pending = []


SLOTS = 96


def exchange_body(
    map_ref, live_ref, parent_ref, upd_ref, panel_ref, bulk_ref, wt_ref,
    upan, turned, top, square, first, second, send_sem, recv_sem, local_sem, part_send, part_recv,
):
    r = lax.axis_index("child")
    j = lax.axis_index("col")
    y, x, zl = j // 8, (j // 2) % 4, j % 2
    t = j % 8
    zh = r // 2
    core = r % 2
    links = Links(send_sem, recv_sem)
    is_root = (r == 0) & (j == 0)

    def col_at(ny, nx, nz):
        return ny * 8 + nx * 2 + nz

    def x_dev(step):
        return (r, col_at(y, (x + step) % 4, zl))

    def y_dev(step):
        return (r, col_at((y + step) % 4, x, zl))

    other_core = (r + 1 - 2 * core, j)

    panel_slots = [links.slot() for _ in range(4)]
    strip = upd_ref.at[0, :, pl.ds(0, 512)]
    for c in range(1, 4):
        @pl.when(r == c)
        def _(c=c):
            links.copy(panel_slots[c], strip, upan.at[c], (0, j)).start()

    bulk_slots = [links.slot() for _ in range(3)]
    partners = [r + 1 - 2 * core, (r + 2) % 4, 3 - r]

    def bulk_send(n):
        def ends():
            rows = pl.ds(pl.multiple_of(partners[n] * 2048, 2048), 2048)
            return upd_ref.at[0, :, rows], bulk_ref.at[r], (partners[n], j)

        links.send(bulk_slots[n], ends)

    own_rows = pl.ds(pl.multiple_of(r * 2048, 2048), 2048)
    own_bulk = pltpu.make_async_copy(upd_ref.at[0, :, own_rows], bulk_ref.at[r], local_sem.at[0])
    bulk_send(0)
    own_bulk.start()

    scatter_slots = [links.slot() for _ in range(4)]
    share_slots = [links.slot() for _ in range(3)]
    corner_slot = links.slot()

    def panel_part(piece, ny):
        return panel_ref.at[piece, ny]

    @pl.when(r == 0)
    def _():
        own = pltpu.make_async_copy(strip, upan.at[0], local_sem.at[1])
        head = pltpu.make_async_copy(parent_ref.at[pl.ds(0, 1024), :], top, local_sem.at[2])
        own.start()
        head.start()
        own.wait()
        for c in range(1, 4):
            links.landed(panel_slots[c], upan.at[c], (c, j))
        for c in range(4):
            for q in range(2):
                for p in range(4):
                    turned[c, p * 128:(p + 1) * 128, q * 128:(q + 1) * 128] = upan[
                        c, q * 128:(q + 1) * 128, p * 128:(p + 1) * 128
                    ].T
        head.wait()

        def place(step, _):
            a, b = step // 4, step % 4
            group = a // 4
            rows = pl.ds(pl.multiple_of(a * 128, 128), 128)
            cols = pl.ds(pl.multiple_of(b * 128, 128), 128)
            total = top[rows, cols]
            for c in range(4):
                for p in range(2):
                    row = 2 * group + p
                    row_weight = jnp.where(map_ref[c, row] == a, live_ref[c, row], 0)
                    source = pl.ds(pl.multiple_of(row * 128, 128), 128)
                    for q in range(2):
                        col = 2 * j + q
                        col_weight = jnp.where(map_ref[c, col] == 4 * j + b, live_ref[c, col], 0)
                        weight = (row_weight * col_weight).astype(jnp.float32)
                        total = total + weight * turned[c, source, q * 128:(q + 1) * 128]
            top[rows, cols] = total
            return 0

        lax.fori_loop(0, 32, place, 0)

    here = (r == 0) & (y == 0)

    @pl.when(here)
    def _():
        pltpu.make_async_copy(top.at[pl.ds(0, 256), :], panel_part(t, 0), local_sem.at[3]).start()

    for n in range(4):
        @pl.when((r == 0) & ((y + n) > 0))
        def _(n=n):
            links.copy(scatter_slots[n], top.at[pl.ds(n * 256, 256), :], panel_part(t, n), (y, n * 8 + t)).start()

    @pl.when((r == 0) & (j == 1))
    def _():
        links.copy(
            corner_slot, top.at[pl.ds(512, 512), :], square.at[pl.ds(512, 512), pl.ds(512, 512)], (0, 0)
        ).start()

    @pl.when(here)
    def _():
        pltpu.make_async_copy(top.at[pl.ds(0, 256), :], panel_part(t, 0), local_sem.at[3]).wait()

    for n in range(4):
        @pl.when((y == n) & ((r + y) > 0))
        def _(n=n):
            links.landed(scatter_slots[n], panel_part(t, n), (0, 8 * r + t))

    pair_slot = links.slot()
    links.send(pair_slot, lambda: (panel_part(t, y), panel_part(t, y), (r, j + 1 - 2 * zl)))

    @pl.when(r == 0)
    def _():
        links.copy(share_slots[0], top, top, (1, j)).start()
        links.copy(share_slots[1], top, top, (2, j)).start()

    @pl.when(is_root)
    def _():
        square[:, 0:512] = top[...]
        for a in range(4):
            for b in range(4):
                square[a * 128:(a + 1) * 128, 512 + b * 128:640 + b * 128] = top[
                    512 + b * 128:640 + b * 128, a * 128:(a + 1) * 128
                ].T
        links.landed(corner_slot, square.at[pl.ds(512, 512), pl.ds(512, 512)], (0, 1))

    OFFSETS = (0, 3, 1, 2)

    def pass_on(slot, region, device):
        def ends():
            here_and_there = region()
            return here_and_there, here_and_there, device()

        links.send(slot, ends)

    def item(kind, nx, ny):
        return panel_ref.at[pl.ds(2 * nx, 2), ny, pl.ds(kind * 128, 128), :]

    def half(kind, nx, ny, h):
        return panel_ref.at[2 * nx + h, ny, pl.ds(kind * 128, 128), :]

    def spot(kind, along, across):
        if kind == 0:
            return (x + along) % 4, (y + across) % 4
        return (x + across) % 4, (y + along) % 4

    def first_dev(kind, step):
        return x_dev(step) if kind == 0 else y_dev(step)

    def second_dev(kind, step):
        return y_dev(step) if kind == 0 else x_dev(step)

    one = [[links.slot() for _ in range(4)] for _ in range(2)]
    two = [{o: [links.slot() for _ in range(4)] for o in OFFSETS} for _ in range(2)]

    def second_send(o):
        for kind in range(2):
            region = lambda kind=kind: item(kind, *spot(kind, o, 0))
            pass_on(two[kind][o][0], region, functools.partial(second_dev, kind, 1))
            pass_on(two[kind][o][1], region, functools.partial(second_dev, kind, 3))

    def second_forward(o):
        for kind in range(2):
            links.landed(two[kind][o][0], item(kind, *spot(kind, o, 3)), second_dev(kind, 3))
            region = lambda kind=kind: half(kind, *spot(kind, o, 3), 0)
            pass_on(two[kind][o][2], region, functools.partial(second_dev, kind, 1))
            links.landed(two[kind][o][1], item(kind, *spot(kind, o, 1)), second_dev(kind, 1))
            region = lambda kind=kind: half(kind, *spot(kind, o, 1), 1)
            pass_on(two[kind][o][3], region, functools.partial(second_dev, kind, 3))

    def second_end(o):
        for kind in range(2):
            links.landed(two[kind][o][2], half(kind, *spot(kind, o, 2), 0), second_dev(kind, 3))
            links.landed(two[kind][o][3], half(kind, *spot(kind, o, 2), 1), second_dev(kind, 1))

    def event_pair():
        links.landed(pair_slot, panel_part(t + 1 - 2 * zl, y), (r, j + 1 - 2 * zl))
        for kind in range(2):
            region = functools.partial(item, kind, x, y)
            pass_on(one[kind][0], region, functools.partial(first_dev, kind, 1))
            pass_on(one[kind][1], region, functools.partial(first_dev, kind, 3))
        second_send(0)
        bulk_send(1)
        bulk_send(2)

    def event_near():
        for kind in range(2):
            links.landed(one[kind][0], item(kind, *spot(kind, 3, 0)), first_dev(kind, 3))
            region = lambda kind=kind: half(kind, *spot(kind, 3, 0), 0)
            pass_on(one[kind][2], region, functools.partial(first_dev, kind, 1))
            links.landed(one[kind][1], item(kind, *spot(kind, 1, 0)), first_dev(kind, 1))
            region = lambda kind=kind: half(kind, *spot(kind, 1, 0), 1)
            pass_on(one[kind][3], region, functools.partial(first_dev, kind, 3))
        second_send(3)
        second_send(1)

    def event_far():
        for kind in range(2):
            links.landed(one[kind][2], half(kind, *spot(kind, 2, 0), 0), first_dev(kind, 3))
            links.landed(one[kind][3], half(kind, *spot(kind, 2, 0), 1), first_dev(kind, 1))
        second_send(2)

    z = zh * 2 + zl
    part = y * 16 + x * 4 + z
    sets = (first, second)
    ring = [[links.slot() for _ in range(9)] for _ in range(2)]
    core_slots = [links.slot() for _ in range(2)]

    def chip(ny, nx, nz):
        return (2 * (nz // 2), col_at(ny, nx, nz % 2))

    def inverse_scatter(n):
        @pl.when(is_root)
        def _():
            def go(s, _):
                piece = sets[n].at[pl.ds(s, 1)]
                pltpu.make_async_remote_copy(
                    src_ref=piece, dst_ref=piece, send_sem=part_send.at[n, s], recv_sem=part_recv.at[n],
                    device_id=chip(s // 16, (s // 4) % 4, s % 4), device_id_type=MESH,
                ).start()
                return 0

            lax.fori_loop(1, 64, go, 0)

    def inverse_scatter_end(n):
        @pl.when(is_root)
        def _():
            def go(s, _):
                piece = sets[n].at[pl.ds(s, 1)]
                pltpu.make_async_remote_copy(
                    src_ref=piece, dst_ref=piece, send_sem=part_send.at[n, s], recv_sem=part_recv.at[n],
                    device_id=chip(s // 16, (s // 4) % 4, s % 4), device_id_type=MESH,
                ).wait_send()
                return 0

            lax.fori_loop(1, 64, go, 0)

    def span(n, level, nz, nx, ny):
        if level == 0:
            return sets[n].at[pl.ds(ny * 16 + nx * 4 + nz, 1)]
        if level == 1:
            return sets[n].at[pl.ds(ny * 16 + nx * 4, 4)]
        return sets[n].at[pl.ds(ny * 16, 16)]

    def moved(level, step):
        if level == 0:
            return (z + step) % 4, x, y
        if level == 1:
            return z, (x + step) % 4, y
        return z, x, (y + step) % 4

    def level_copies(n, level, act):
        for step in range(1, 4):
            nz, nx, ny = moved(level, step)

            @pl.when((core == 0) & (nz + nx + ny > 0))
            def _(step=step, nz=nz, nx=nx, ny=ny):
                region = span(n, level, z, x, y)
                act(links.copy(ring[n][level * 3 + step - 1], region, region, chip(ny, nx, nz)))

    def level_send(n, level):
        level_copies(n, level, lambda copy: copy.start())

    def level_end(n, level):
        @pl.when((core == 0) & (part > 0))
        def _():
            for step in range(1, 4):
                nz, nx, ny = moved(level, 4 - step)
                links.landed(ring[n][level * 3 + step - 1], span(n, level, nz, nx, ny), chip(ny, nx, nz))

    def part_end(n):
        @pl.when((core == 0) & (part > 0))
        def _():
            piece = sets[n].at[pl.ds(part, 1)]
            pltpu.make_async_remote_copy(
                src_ref=piece, dst_ref=piece, send_sem=part_send.at[n, 0], recv_sem=part_recv.at[n],
                device_id=(0, 0), device_id_type=MESH,
            ).wait_recv()

    def core_send(n):
        @pl.when(core == 0)
        def _():
            links.copy(core_slots[n], sets[n], sets[n], (r + 1, j)).start()

    def core_end(n):
        @pl.when(core == 1)
        def _():
            links.landed(core_slots[n], sets[n], (r - 1, j))

    def event_share():
        @pl.when(r == 1)
        def _():
            links.landed(share_slots[0], top, (0, j))

        @pl.when(r == 2)
        def _():
            links.landed(share_slots[1], top, (0, j))
            links.copy(share_slots[2], top, top, (3, j)).start()

        @pl.when(r == 3)
        def _():
            links.landed(share_slots[2], top, (2, j))

    def times(a, b, dims):
        return lax.dot_general(a, b, (dims, ((), ())), precision=HIGHEST, preferred_element_type=jnp.float32)

    def weights_first():
        wt_ref[:, 512:1024] = jnp.zeros((512, 512), jnp.float32)

        @pl.when(j == 0)
        def _():
            wt_ref[:, 0:512] = first[...].reshape(512, 512)

        @pl.when(j == 1)
        def _():
            wt_ref[:, 0:512] = jnp.zeros((512, 512), jnp.float32)

        @pl.when(j >= 2)
        def _():
            inverse = first[...].reshape(512, 512)
            solved = times(inverse, top[0:512, :], ((1,), (0,)))
            wt_ref[:, 0:512] = -times(solved, inverse, ((0,), (0,)))

    def weights_second():
        @pl.when(j == 1)
        def _():
            wt_ref[...] = second[...].reshape(512, 1024)

        @pl.when(j >= 2)
        def _():
            inverse = second[...].reshape(512, 1024)
            solved = times(inverse, top[...], ((1,), (0,)))
            wt_ref[...] = wt_ref[...] - times(solved, inverse, ((0,), (0,)))

    def keep_inverse(n):
        @pl.when(is_root)
        def _():
            width = 512 * (n + 1)
            rows = n * 512 + lax.broadcasted_iota(jnp.int32, (512, width), 0)
            cols = lax.broadcasted_iota(jnp.int32, (512, width), 1)
            kept = jnp.where(cols <= rows, square[n * 512:(n + 1) * 512, 0:width], 0.0)
            sets[n][...] = kept.reshape(64, 8, width)

    plan = {
        0: [event_pair],
        1: [],
        2: [event_near],
        3: [functools.partial(keep_inverse, 0), functools.partial(inverse_scatter, 0), event_far, event_share],
        4: [functools.partial(part_end, 0), functools.partial(level_send, 0, 0),
            functools.partial(second_forward, 0),
            functools.partial(level_end, 0, 0), functools.partial(level_send, 0, 1)],
        5: [functools.partial(second_forward, 3), functools.partial(second_forward, 1),
            functools.partial(level_end, 0, 1), functools.partial(level_send, 0, 2)],
        6: [functools.partial(second_forward, 2),
            functools.partial(level_end, 0, 2), functools.partial(core_send, 0),
            functools.partial(core_end, 0), weights_first],
        7: [functools.partial(keep_inverse, 1), functools.partial(inverse_scatter, 1)],
    }

    def step(k, _):
        @pl.when(is_root)
        def _():
            factor_step(square, k)

        for n, events in plan.items():
            if events:
                @pl.when(k == n)
                def _(events=events):
                    for event in events:
                        event()

        return 0

    lax.fori_loop(0, 8, step, 0)
    part_end(1)
    level_send(1, 0)
    level_end(1, 0)
    level_send(1, 1)
    level_end(1, 1)
    level_send(1, 2)
    level_end(1, 2)
    core_send(1)
    core_end(1)
    weights_second()
    for o in OFFSETS:
        second_end(o)
    own_bulk.wait()
    for n in range(3):
        links.landed(bulk_slots[n], bulk_ref.at[partners[n]], (partners[n], j))
    links.drain()
    for c in range(1, 4):
        @pl.when(r == c)
        def _(c=c):
            links.copy(panel_slots[c], strip, upan.at[c], (0, j)).wait_send()
    for n in range(4):
        @pl.when((r == 0) & ((y + n) > 0))
        def _(n=n):
            links.copy(scatter_slots[n], top.at[pl.ds(n * 256, 256), :], panel_part(t, n), (y, n * 8 + t)).wait_send()

    @pl.when((r == 0) & (j == 1))
    def _():
        links.copy(
            corner_slot, top.at[pl.ds(512, 512), :], square.at[pl.ds(512, 512), pl.ds(512, 512)], (0, 0)
        ).wait_send()

    @pl.when(r == 0)
    def _():
        links.copy(share_slots[0], top, top, (1, j)).wait_send()
        links.copy(share_slots[1], top, top, (2, j)).wait_send()

    @pl.when(r == 2)
    def _():
        links.copy(share_slots[2], top, top, (3, j)).wait_send()

    for n in range(2):
        inverse_scatter_end(n)

        for level in range(3):
            level_copies(n, level, lambda copy: copy.wait_send())

        @pl.when(core == 0)
        def _(n=n):
            links.copy(core_slots[n], sets[n], sets[n], (r + 1, j)).wait_send()


def exchange(maps, live, parent, updates):
    hbm = pl.BlockSpec(memory_space=pl.ANY)
    smem = pl.BlockSpec(memory_space=pltpu.SMEM)
    return pl.pallas_call(
        exchange_body,
        out_shape=(
            jax.ShapeDtypeStruct((8, 4, 256, 512), jnp.float32),
            jax.ShapeDtypeStruct((4, 256, 2048), jnp.float32),
            jax.ShapeDtypeStruct((512, 1024), jnp.float32),
        ),
        in_specs=[smem, smem, hbm, hbm],
        out_specs=(hbm, hbm, pl.BlockSpec(memory_space=pltpu.VMEM)),
        scratch_shapes=[
            pltpu.VMEM((4, 256, 512), jnp.float32),
            pltpu.VMEM((4, 512, 256), jnp.float32),
            pltpu.VMEM((1024, 512), jnp.float32),
            pltpu.VMEM((1024, 1024), jnp.float32),
            pltpu.VMEM((64, 8, 512), jnp.float32),
            pltpu.VMEM((64, 8, 1024), jnp.float32),
            pltpu.SemaphoreType.DMA((SLOTS,)),
            pltpu.SemaphoreType.DMA((SLOTS,)),
            pltpu.SemaphoreType.DMA((4,)),
            pltpu.SemaphoreType.DMA((2, 64)),
            pltpu.SemaphoreType.DMA((2,)),
        ],
        compiler_params=pltpu.CompilerParams(has_side_effects=True, vmem_limit_bytes=40 * 2**20),
    )(maps, live, parent, updates)


def per_device(parent, updates, maps, live):
    panel, bulk, wt = exchange(maps, live, parent, updates)
    place = jnp.stack([lax.axis_index("child"), lax.axis_index("col")]).astype(jnp.int32)
    return finish(place, maps, live, parent, bulk, panel.reshape(8, 1024, 512), wt)


def solution(mesh):
    in_specs = (P("child", "col"), P("child", "col", None), P(), P())
    return jax.shard_map(
        per_device, mesh=mesh, in_specs=in_specs, out_specs=P("child", "col"), check_vma=False
    )
```

time: 1580 us -> 268 us (0.17)
  waiting for transfers between devices: 949 us -> 0 us
  Pallas kernels: 0 us -> 261 us
  other arithmetic: 254 us -> 0.07 us
  matrix products: 158 us -> 0 us
  blocking collectives: 101 us -> 0 us
  local copies, waits for them, and re-layouts: 84.5 us -> 4.59 us
  between operations: 18.8 us -> 0.02 us
    psum x4 -> x0, waiting for transfers between devices: 864 us -> none  [spread(): return lax.psum(block, axis)]
    pallas_call x0 -> x2, Pallas kernels: none -> 261 us  [the longest x1 237 us: exchange(): pl.pallas_call(exchange_body, out_shape=(jax.ShapeDtypeStruct((8, 4, 256,...]
    another operation x34 -> x1, other arithmetic: 237 us -> 0.07 us  [per_device(): jnp.stack([lax.axis_index('child'), lax.axis_index('col')])]
    dot_general x8 -> x0, matrix products: 148 us -> none  [the longest x2 53.7 us: per_device(): matrix = matrix - jnp.dot(factor * row_keep, side_rows.T, precision=HIGHEST)]
    all_to_all x1 -> x0, blocking collectives: 101 us -> none  [per_device(): lax.all_to_all(updates[0], 'col', split_axis=1, concat_axis=0, tiled=True)]
    all_to_all x1 -> x0, waiting for transfers between devices: 84.4 us -> none  [per_device(): lax.all_to_all(lax.all_to_all(updates[0], 'col', split_axis=1, concat_axi...]
    another operation x39 -> x0, local copies, waits for them, and re-layouts: 21.2 us -> none  [the longest x27 15.7 us: inverse_factor(): lax.linalg.triangular_solve(lower_part, identity, left_side=True, lower=T...]
    reshape x2 -> x0, local copies, waits for them, and re-layouts: 19.7 us -> none  [the longest x1 10.8 us: per_device(): gathered = by_owner.reshape(groups, tile_count, BLOCK, pair_count, BLOCK)]
  transfers between devices with their start and end apart: 5 -> 0, of which waited for: 5 -> 0; matrix products, arithmetic and copies ran while one was open for 1% -> 0% of each run, Pallas kernels for 0% -> 0%
where the time goes in v1:
time: 268 us; the launch traced here: 266 us
  Pallas kernels  261 us (97%)
  local copies, waits for them, and re-layouts  4.59 us (2%)
    pallas_call x1, Pallas kernels, exchange(): pl.pallas_call(exchange_body, out_shape=(jax.ShapeDtypeStruct((8, 4, 256,...  237 us
    pallas_call x1, Pallas kernels, finish(): pl.pallas_call(finish_body, grid_spec=spec, out_shape=jax.ShapeDtypeStruc...  23.9 us

profile of v1, /device:TPU:37, one launch (start us, length us, event | category | flops | bytes accessed | tf_op | source)
XLA Modules:
  0.0 265.9 jit_solution(14786932156211321160)
XLA Ops:
  0.0 0.1 pad_add_fusion.place_ref
  0.1 0.0 copy-start
  0.1 0.7 copy-done
  0.8 0.0 copy-start.2
  0.8 0.7 copy-done.2
  1.4 0.0 copy-start.1
  1.4 0.0 copy-start.3
  1.4 237.3 %shard_map.46 = (f32[8,4,256,512]{3,2,1,0:T(8,128)}, f32[4,256,2048]{2,1,0:T(8,128)S(1)}, f32[512,1024]{1,0:T(8,128)S(1)}) custom-call(s32[4,64]{1,0:T(4,128)S(1)} %copy-done, s32[4,64]{1,0:T(4,128)S(1)} %copy-done.2, f32[4096,512]{1,0:T(8,128)} %parent_ref.3, f32[1,256,8192]{2,1,0:T(8,128)} %upd_ref.1), custom_call_target="tpu_custom_call" | custom-call | tf_op jit(solution)/shard_map/pallas_call | solution.py:590
  238.8 0.0 copy-start.4
  238.8 3.2 %copy-done.4 = f32[4,256,2048]{2,1,0:T(8,128)} copy-done((f32[4,256,2048]{2,1,0:T(8,128)}, f32[4,256,2048]{2,1,0:T(8,128)S(1)}, u32[]{:S(2)}) %copy-start.4) | copy-done | bytes 8388632
  242.0 0.0 copy-done.1
  242.0 0.0 copy-done.3
  242.0 23.9 %shard_map.47 = f32[4096,512]{1,0:T(8,128)} custom-call(s32[2]{0:T(128)S(1)} %pad_add_fusion.place_ref, s32[4,64]{1,0:T(4,128)S(1)} %copy-done.1, s32[4,64]{1,0:T(4,128)S(1)} %copy-done.3, f32[4096,512]{1,0:T(8,128)} %parent_ref.3, f32[4,256,2048]{2,1,0:T(8,128)} %copy-done.4, f32[8,1024,512]{2,1,0:T(8,128)} %bitcast.3, f32[512,1024]{1,0:T(8,128)S(1)} %get-tuple-element.10.wt_ref), custom_call_target="tpu_custom_call" | custom-call | flops 12884901888 | bytes 47185920 | tf_op jit(solution)/shard_map/pallas_call | solution.py:110
Async XLA Ops:
  0.1 0.7 copy-start
  0.8 0.7 copy-start.2
  1.4 240.6 %copy-start.1 = (s32[4,64]{1,0:T(4,128)S(1)}, s32[4,64]{1,0:T(4,128)}, u32[]{:S(2)}) copy-start(s32[4,64]{1,0:T(4,128)} %map_ref.3) | copy-start | bytes 3076
  1.4 240.6 %copy-start.3 = (s32[4,64]{1,0:T(4,128)S(1)}, s32[4,64]{1,0:T(4,128)}, u32[]{:S(2)}) copy-start(s32[4,64]{1,0:T(4,128)} %live_ref.3) | copy-start | bytes 3076
  238.8 3.2 %copy-start.4 = (f32[4,256,2048]{2,1,0:T(8,128)}, f32[4,256,2048]{2,1,0:T(8,128)S(1)}, u32[]{:S(2)}) copy-start(f32[4,256,2048]{2,1,0:T(8,128)S(1)} %get-tuple-element.8.upd_ref) | copy-start | bytes 25165828

commit v2 on v1

v2 whole, which is shorter than its diff:
```python
import functools

import jax
import jax.numpy as jnp
from jax import lax
from jax.experimental import pallas as pl
from jax.experimental.pallas import tpu as pltpu
from jax.sharding import PartitionSpec as P

HIGHEST = lax.Precision.HIGHEST


def recip(d):
    r = pl.reciprocal(d, approx=True)
    return r*(2.0-d*r)
def rsq(d):
    r = lax.rsqrt(d)
    return r*(1.5-0.5*d*r*r)
def diag_inverse(tile):
    rows=[tile[8*g:8*g+8,:] for g in range(16)]
    lane=lax.broadcasted_iota(jnp.int32,(8,128),1)
    sub=lax.broadcasted_iota(jnp.int32,(8,128),0)
    wide=lambda v: jnp.broadcast_to(v,(8,128))
    for m in range(16):
        o=8*m
        V=rows[m]
        inside=(lane>=o)&(lane<o+8)
        b={(i,q): wide(V[i:i+1,o+q:o+q+1]) for i in range(8) for q in range(i+1)}
        cols={(g,q): wide(rows[g][:,o+q:o+q+1]) for g in range(m+1,16) for q in range(8)}
        V=jnp.where(inside, jnp.where(lane-o==sub,1.0,0.0), V)
        v=[wide(V[i:i+1,:]) for i in range(8)]
        if m<15:
            after=jnp.where(inside,0.0,rows[m+1])
            ce=[cols[m+1,q] for q in range(8)]
        l={}; rd=[]
        for q in range(8):
            rd.append(recip(b[q,q]))
            for i in range(q+1,8):
                for c in range(q+1,i+1):
                    b[i,c]=b[i,c]-(b[i,q]*b[c,q])*rd[q]
                l[i,q]=b[i,q]*rd[q]
                v[i]=v[i]-l[i,q]*v[q]
            if m<15:
                times=ce[q]*rd[q]
                after=after-times*v[q]
                for c in range(q+1,8):
                    ce[c]=ce[c]-times*b[c,q]
        if m<15:
            rows[m+1]=after
        new=v[0]*rsq(b[0,0])
        for i in range(1,8):
            new=jnp.where(sub==i, v[i]*rsq(b[i,i]), new)
        rows[m]=new
        if m<14:
            t=[v[i]*rd[i] for i in range(8)]
            for i in range(6,-1,-1):
                for c in range(i+1,8):
                    t[i]=t[i]-l[c,i]*t[c]
            for g in range(m+2,16):
                acc=jnp.where(inside,0.0,rows[g])
                for q in range(8):
                    acc=acc-cols[g,q]*t[q]
                rows[g]=acc
    full=jnp.concatenate(rows,0)
    r=lax.broadcasted_iota(jnp.int32,(128,128),0); c=lax.broadcasted_iota(jnp.int32,(128,128),1)
    return jnp.where(c<=r, full, 0.0)
def block_at(k):
    return pl.ds(pl.multiple_of(k*128,128),128)
def factor_start(S,inv):
    inv[...]=diag_inverse(S[0:128,0:128])
def factor_step(S,inv,k):
    at=block_at(k)
    r=lax.broadcasted_iota(jnp.int32,(128,128),0); c=lax.broadcasted_iota(jnp.int32,(128,128),1)
    S[at,at]=jnp.where(r==c,1.0,0.0)
    row=jnp.dot(inv[...],S[at,:],precision=HIGHEST,preferred_element_type=jnp.float32)
    S[at,:]=row
    def clear(i,_):
        S[block_at(i),at]=jnp.zeros((128,128),jnp.float32)
        return 0
    lax.fori_loop(k+1,8,clear,0)
    @pl.when(k<7)
    def _():
        nx=block_at(k+1)
        tn=lambda a,b: lax.dot_general(a,b,(((0,),(0,)),((),())),precision=HIGHEST,preferred_element_type=jnp.float32)
        S[nx,:]=S[nx,:]-tn(S[at,nx],S[at,:])
        tile=S[nx,nx]
        cols=lax.broadcasted_iota(jnp.int32,(128,1024),1)
        full=S[at,:]
        left=jnp.where(cols>=(k+2)*128,full,0.0)
        inv[...]=diag_inverse(tile)
        for g in range(2,8):
            S[g*128:g*128+128,:]=S[g*128:g*128+128,:]-tn(left[:,g*128:g*128+128],full)


def finish_body(place_ref, map_ref, live_ref, parent_ref, upd_ref, panel_ref, wt_ref, out_ref, whi, wlo, acc):
    i=pl.program_id(0)
    r=place_ref[0]; j=place_ref[1]
    @pl.when(i==0)
    def _():
        w=wt_ref[...]
        h=w.astype(jnp.bfloat16)
        whi[...]=h
        wlo[...]=(w-h.astype(jnp.float32)).astype(jnp.bfloat16)
    a=panel_ref[0]
    ahi=a.astype(jnp.bfloat16)
    alo=(a-ahi.astype(jnp.float32)).astype(jnp.bfloat16)
    dot=lambda x,y: jnp.dot(x,y,preferred_element_type=jnp.float32)
    acc[...]=dot(whi[...],ahi)+(dot(whi[...],alo)+dot(wlo[...],ahi))
    keep=jnp.where(j>=2,1.0,0.0).astype(jnp.float32)
    for c in range(4):
        for q in range(2):
            col=2*j+q
            bq=map_ref[c,col]-4*j
            lq=live_ref[c,col].astype(jnp.float32)*keep
            for p in range(2):
                row=16*r+2*i+p
                ap=map_ref[c,row]-4*(8*r+i)
                w=lq*live_ref[c,row].astype(jnp.float32)
                dst=(pl.ds(pl.multiple_of(bq*128,128),128),pl.ds(pl.multiple_of(ap*128,128),128))
                acc[dst]=acc[dst]+w*upd_ref[c,q*128:q*128+128,p*128:p*128+128]
    total=acc[...].T+keep*parent_ref[...]
    g=r*4096+i*512+lax.broadcasted_iota(jnp.int32,(512,512),0)
    s=j*512+lax.broadcasted_iota(jnp.int32,(512,512),1)
    out_ref[...]=jnp.where(g<jnp.minimum(s,1024),0.0,total)
def finish(place,maps,live,parent,upd,panel,wt):
    spec=pltpu.PrefetchScalarGridSpec(num_scalar_prefetch=3,grid=(8,),
      in_specs=[pl.BlockSpec((512,512),lambda i,*_:(i,0)),
                pl.BlockSpec((4,256,256),lambda i,*_:(0,0,i)),
                pl.BlockSpec((1,1024,512),lambda i,*_:(i,0,0)),
                pl.BlockSpec((512,1024),lambda i,*_:(0,0))],
      out_specs=pl.BlockSpec((512,512),lambda i,*_:(i,0)),
      scratch_shapes=[pltpu.VMEM((512,1024),jnp.bfloat16),pltpu.VMEM((512,1024),jnp.bfloat16),pltpu.VMEM((512,512),jnp.float32)])
    return pl.pallas_call(finish_body,grid_spec=spec,out_shape=jax.ShapeDtypeStruct((4096,512),jnp.float32),
      compiler_params=pltpu.CompilerParams(vmem_limit_bytes=48*2**20),
      cost_estimate=pl.CostEstimate(flops=3*2*4096*512*1024,bytes_accessed=45*2**20,transcendentals=0))(place,maps,live,parent,upd,panel,wt)


MESH = pl.DeviceIdType.MESH


class Links:
    def __init__(self, send_sem, recv_sem):
        self.send_sem, self.recv_sem, self.used = send_sem, recv_sem, 0
        self.pending = []

    def slot(self):
        self.used += 1
        return self.used - 1

    def slots(self, count):
        self.used += count
        return self.used - count

    def copy(self, slot, source, target, device):
        return pltpu.make_async_remote_copy(
            src_ref=source,
            dst_ref=target,
            send_sem=self.send_sem.at[slot],
            recv_sem=self.recv_sem.at[slot],
            device_id=device,
            device_id_type=MESH,
        )

    def send(self, slot, ends):
        self.copy(slot, *ends()).start()
        self.pending.append((slot, ends))

    def landed(self, slot, region, device):
        self.copy(slot, region, region, device).wait_recv()

    def drain(self):
        for slot, ends in self.pending:
            self.copy(slot, *ends()).wait_send()
        self.pending = []


SLOTS = 128
BULK = (0, 2, 1, 2, 1, 2)
WIDTHS = (768, 512)
WHERE = ((0, 0), (0, 128), (0, 384), (1, 0))


def exchange_body(
    map_ref, live_ref, parent_ref, upd_ref, panel_ref, bulk_ref, wt_ref,
    raw, turned, chunk, top, square, corner, inverse, weight, set_0, set_1,
    send_sem, recv_sem, local_sem, part_send, part_recv,
):
    r = lax.axis_index("child")
    j = lax.axis_index("col")
    y, x, zl = j // 8, (j // 2) % 4, j % 2
    t = j % 8
    zh = r // 2
    core = r % 2
    links = Links(send_sem, recv_sem)
    is_root = (r == 0) & (j == 0)
    source_col = 8 * r + t

    def col_at(ny, nx, nz):
        return ny * 8 + nx * 2 + nz

    def x_dev(step):
        return (r, col_at(y, (x + step) % 4, zl))

    def y_dev(step):
        return (r, col_at((y + step) % 4, x, zl))

    def panel_part(piece, ny):
        return panel_ref.at[piece, ny]

    head_slot = links.slots(4)
    strip_slot = links.slots(16)

    def strip(n):
        return upd_ref.at[0, :, pl.ds(256 * (n // 2), 256)]

    def head_copy(n):
        return links.copy(head_slot + n, parent_ref.at[pl.ds(256 * n, 256), :], chunk, (y, n * 8 + t))

    def strip_copy(n):
        return links.copy(strip_slot + 4 * r + n, strip(n), raw.at[r], (y, n * 8 + t))

    def panel_sends(act):
        for n in range(4):
            @pl.when((r != y) | (y != n))
            def _(n=n):
                act(strip_copy(n))

            @pl.when((r == 0) & (y + n > 0))
            def _(n=n):
                act(head_copy(n))

    panel_sends(lambda copy: copy.start())
    own_head = pltpu.make_async_copy(parent_ref.at[pl.ds(0, 256), :], chunk, local_sem.at[1])

    def own_strip():
        part = upd_ref.at[0, :, pl.ds(pl.multiple_of(256 * (y // 2), 256), 256)]
        return pltpu.make_async_copy(part, raw.at[r], local_sem.at[2])

    @pl.when((r == 0) & (y == 0))
    def _():
        own_head.start()

    @pl.when(r == y)
    def _():
        own_strip().start()

    partners = [r + 1 - 2 * core, (r + 2) % 4, 3 - r]
    bulk_slot = links.slot()
    bulk_queue = [(n, m, links.slot()) for m in range(4) for n in (1, 2)]
    bulk_all = list(bulk_queue)

    def bulk_send():
        def ends():
            rows = pl.ds(pl.multiple_of(partners[0] * 2048, 2048), 2048)
            return upd_ref.at[0, :, rows], bulk_ref.at[r], (partners[0], j)

        links.send(bulk_slot, ends)

    def bulk_some(count):
        for _ in range(count):
            n, m, slot = bulk_queue.pop(0)

            def ends(n=n, m=m):
                rows = pl.ds(pl.multiple_of(partners[n] * 2048 + 512 * m, 512), 512)
                return upd_ref.at[0, :, rows], bulk_ref.at[r, :, pl.ds(512 * m, 512)], (partners[n], j)

            links.send(slot, ends)

    own_rows = pl.ds(pl.multiple_of(r * 2048, 2048), 2048)
    own_bulk = pltpu.make_async_copy(upd_ref.at[0, :, own_rows], bulk_ref.at[r], local_sem.at[0])
    bulk_some(BULK[0])
    weight[...] = jnp.zeros((512, 1024), jnp.float32)

    @pl.when(r == y)
    def _():
        own_strip().wait()

    for c in range(4):
        @pl.when((r != c) | (r != y))
        def _(c=c):
            links.landed(strip_slot + 4 * c + y, raw.at[c], (c, source_col))
        for q in range(2):
            for p in range(2):
                turned[c, p * 128:(p + 1) * 128, q * 128:(q + 1) * 128] = raw[
                    c, q * 128:(q + 1) * 128, p * 128:(p + 1) * 128
                ].T

    @pl.when((r == 0) & (y == 0))
    def _():
        own_head.wait()

    @pl.when((r > 0) | (y > 0))
    def _():
        links.landed(head_slot + y, chunk, (0, source_col))

    def place(step, _):
        a, b = step // 4, step % 4
        rows = pl.ds(pl.multiple_of(a * 128, 128), 128)
        cols = pl.ds(pl.multiple_of(b * 128, 128), 128)
        total = chunk[rows, cols]
        for c in range(4):
            for p in range(2):
                row = 2 * (y // 2) + p
                row_weight = jnp.where(map_ref[c, row] == 2 * y + a, live_ref[c, row], 0)
                for q in range(2):
                    col = 2 * source_col + q
                    col_weight = jnp.where(map_ref[c, col] == 4 * source_col + b, live_ref[c, col], 0)
                    both = (row_weight * col_weight).astype(jnp.float32)
                    total = total + both * turned[c, p * 128:(p + 1) * 128, q * 128:(q + 1) * 128]
        chunk[rows, cols] = total
        return 0

    lax.fori_loop(0, 8, place, 0)

    pivot_slot = links.slots(8)

    def pivot_part(side, n):
        if side == 0:
            return square.at[pl.ds(pl.multiple_of(n * 256, 256), 256), pl.ds(0, 512)]
        return corner.at[pl.ds(pl.multiple_of(n * 256 - 512, 256), 256), :]

    def pivot_sends(act):
        for side in range(2):
            @pl.when((r == 0) & (t == side) & (y > side))
            def _(side=side):
                act(links.copy(pivot_slot + 4 * side + y, chunk, pivot_part(side, y), (0, 0)))

    pivot_sends(lambda copy: copy.start())
    pair_slot = links.slot()
    links.send(pair_slot, lambda: (chunk, panel_part(t, y), (r, j + 1 - 2 * zl)))
    own_chunk = pltpu.make_async_copy(chunk, panel_part(t, y), local_sem.at[1])
    own_chunk.start()
    bulk_send()
    own_bulk.start()

    def root_square():
        square[0:256, 0:512] = chunk[...]
        square[512:1024, 512:1024] = jnp.zeros((512, 512), jnp.float32)
        for n in range(1, 4):
            links.landed(pivot_slot + n, pivot_part(0, n), (0, 8 * n))
        for a in range(4):
            for b in range(4):
                square[a * 128:(a + 1) * 128, 512 + b * 128:640 + b * 128] = square[
                    512 + b * 128:640 + b * 128, a * 128:(a + 1) * 128
                ].T
        factor_start(square, inverse)

    def root_corner():
        for n in range(2, 4):
            links.landed(pivot_slot + 4 + n, pivot_part(1, n), (0, 8 * n + 1))
        square[512:1024, 512:1024] = square[512:1024, 512:1024] + corner[...]

    OFFSETS = (0, 3, 1, 2)

    def pass_on(slot, region, device):
        def ends():
            here_and_there = region()
            return here_and_there, here_and_there, device()

        links.send(slot, ends)

    def item(kind, nx, ny):
        return panel_ref.at[pl.ds(2 * nx, 2), ny, pl.ds(kind * 128, 128), :]

    def half(kind, nx, ny, h):
        return panel_ref.at[2 * nx + h, ny, pl.ds(kind * 128, 128), :]

    def spot(kind, along, across):
        if kind == 0:
            return (x + along) % 4, (y + across) % 4
        return (x + across) % 4, (y + along) % 4

    def first_dev(kind, step):
        return x_dev(step) if kind == 0 else y_dev(step)

    def second_dev(kind, step):
        return y_dev(step) if kind == 0 else x_dev(step)

    one = [[links.slot() for _ in range(4)] for _ in range(2)]
    two = [{o: [links.slot() for _ in range(4)] for o in OFFSETS} for _ in range(2)]

    def second_send(o):
        for kind in range(2):
            region = lambda kind=kind: item(kind, *spot(kind, o, 0))
            pass_on(two[kind][o][0], region, functools.partial(second_dev, kind, 1))
            pass_on(two[kind][o][1], region, functools.partial(second_dev, kind, 3))

    def second_forward(o):
        for kind in range(2):
            links.landed(two[kind][o][0], item(kind, *spot(kind, o, 3)), second_dev(kind, 3))
            region = lambda kind=kind: half(kind, *spot(kind, o, 3), 0)
            pass_on(two[kind][o][2], region, functools.partial(second_dev, kind, 1))
            links.landed(two[kind][o][1], item(kind, *spot(kind, o, 1)), second_dev(kind, 1))
            region = lambda kind=kind: half(kind, *spot(kind, o, 1), 1)
            pass_on(two[kind][o][3], region, functools.partial(second_dev, kind, 3))

    def second_end(o):
        for kind in range(2):
            links.landed(two[kind][o][2], half(kind, *spot(kind, o, 2), 0), second_dev(kind, 3))
            links.landed(two[kind][o][3], half(kind, *spot(kind, o, 2), 1), second_dev(kind, 1))

    def event_pair():
        own_chunk.wait()
        links.landed(pair_slot, panel_part(t + 1 - 2 * zl, y), (r, j + 1 - 2 * zl))
        for kind in range(2):
            region = functools.partial(item, kind, x, y)
            pass_on(one[kind][0], region, functools.partial(first_dev, kind, 1))
            pass_on(one[kind][1], region, functools.partial(first_dev, kind, 3))
        second_send(0)
        bulk_some(BULK[1])

    def event_near():
        for kind in range(2):
            links.landed(one[kind][0], item(kind, *spot(kind, 3, 0)), first_dev(kind, 3))
            region = lambda kind=kind: half(kind, *spot(kind, 3, 0), 0)
            pass_on(one[kind][2], region, functools.partial(first_dev, kind, 1))
            links.landed(one[kind][1], item(kind, *spot(kind, 1, 0)), first_dev(kind, 1))
            region = lambda kind=kind: half(kind, *spot(kind, 1, 0), 1)
            pass_on(one[kind][3], region, functools.partial(first_dev, kind, 3))
        second_send(3)
        second_send(1)

    def event_far():
        for kind in range(2):
            links.landed(one[kind][2], half(kind, *spot(kind, 2, 0), 0), first_dev(kind, 3))
            links.landed(one[kind][3], half(kind, *spot(kind, 2, 0), 1), first_dev(kind, 1))
        second_send(2)

    home = r == y
    across = r == (y + 2) % 4
    home_core = r == y + 1 - 2 * (y % 2)
    share_slots = [links.slot() for _ in range(3)]

    def own_top():
        return pltpu.make_async_copy(panel_ref.at[t], top, local_sem.at[2])

    def share_copies():
        return (
            links.copy(share_slots[0], panel_ref.at[t], top, ((r + 2) % 4, j)),
            links.copy(share_slots[1], panel_ref.at[t], top, (r + 1 - 2 * core, j)),
        )

    def share_core():
        return links.copy(share_slots[2], top, top, (r + 1 - 2 * core, j))

    def event_share():
        second_end(0)

        @pl.when(home)
        def _():
            for copy in share_copies():
                copy.start()
            own_top().start()

    def event_share_across():
        @pl.when(home)
        def _():
            own_top().wait()

        @pl.when(home_core)
        def _():
            links.landed(share_slots[1], top, (y, j))

        @pl.when(across)
        def _():
            links.landed(share_slots[0], top, (y, j))
            share_core().start()

    def event_share_end():
        @pl.when(jnp.logical_not(home | home_core | across))
        def _():
            links.landed(share_slots[2], top, ((y + 2) % 4, j))

    z = zh * 2 + zl
    part = y * 16 + x * 4 + z
    sets = (set_0, set_1)
    ring = [[links.slot() for _ in range(9)] for _ in range(2)]
    core_slots = [links.slot() for _ in range(2)]

    def chip(ny, nx, nz):
        return (2 * (nz // 2), col_at(ny, nx, nz % 2))

    def part_copy(n, s, device):
        piece = sets[n].at[pl.ds(s, 1)]
        return pltpu.make_async_remote_copy(
            src_ref=piece, dst_ref=piece, send_sem=part_send.at[n, s], recv_sem=part_recv.at[n],
            device_id=device, device_id_type=MESH,
        )

    def part_sends(n, act):
        @pl.when(is_root)
        def _():
            def go(s, _):
                act(part_copy(n, s, chip(s // 16, (s // 4) % 4, s % 4)))
                return 0

            lax.fori_loop(1, 64, go, 0)

    def span(n, level, nz, nx, ny):
        if level == 0:
            return sets[n].at[pl.ds(ny * 16 + nx * 4 + nz, 1)]
        if level == 1:
            return sets[n].at[pl.ds(ny * 16 + nx * 4, 4)]
        return sets[n].at[pl.ds(ny * 16, 16)]

    def moved(level, step):
        if level == 0:
            return (z + step) % 4, x, y
        if level == 1:
            return z, (x + step) % 4, y
        return z, x, (y + step) % 4

    def level_copies(n, level, act):
        for step in range(1, 4):
            nz, nx, ny = moved(level, step)

            @pl.when((core == 0) & (nz + nx + ny > 0))
            def _(step=step, nz=nz, nx=nx, ny=ny):
                region = span(n, level, z, x, y)
                act(links.copy(ring[n][level * 3 + step - 1], region, region, chip(ny, nx, nz)))

    def level_end(n, level):
        @pl.when((core == 0) & (part > 0))
        def _():
            for step in range(1, 4):
                nz, nx, ny = moved(level, 4 - step)
                links.landed(ring[n][level * 3 + step - 1], span(n, level, nz, nx, ny), chip(ny, nx, nz))

    def core_copy(n):
        return links.copy(core_slots[n], sets[n], sets[n], (r + 1, j))

    def keep(n):
        half = 128 * (n + 1)
        which, at = WHERE[n]
        rows = n * 256 + lax.broadcasted_iota(jnp.int32, (256, half), 0)
        cols = lax.broadcasted_iota(jnp.int32, (256, half), 1)
        for h in range(2):
            kept = square[n * 256:(n + 1) * 256, h * half:(h + 1) * half]
            kept = jnp.where(cols + h * half <= rows, kept, 0.0)
            sets[which][h * 32:(h + 1) * 32, :, at:at + half] = kept.reshape(32, 8, half)

    def leave(n):
        @pl.when(is_root)
        def _():
            for m in ((0, 1, 2), (3,))[n]:
                keep(m)

        part_sends(n, lambda copy: copy.start())

    def over_z(n):
        @pl.when((core == 0) & (part > 0))
        def _():
            part_copy(n, part, (0, 0)).wait_recv()

        level_copies(n, 0, lambda copy: copy.start())

    def over_x(n):
        level_end(n, 0)
        level_copies(n, 1, lambda copy: copy.start())

    def over_y(n):
        level_end(n, 1)
        level_copies(n, 2, lambda copy: copy.start())

    def over_core(n):
        level_end(n, 2)

        @pl.when(core == 0)
        def _():
            core_copy(n).start()

    def split(a):
        high = a.astype(jnp.bfloat16)
        return high, (a - high.astype(jnp.float32)).astype(jnp.bfloat16)

    def times(a, b, dims):
        dot = lambda u, v: lax.dot_general(u, v, (dims, ((), ())), preferred_element_type=jnp.float32)
        return dot(a[0], b[0]) + (dot(a[0], b[1]) + dot(a[1], b[0]))

    def weigh(n):
        half = 128 * (n + 1)
        which, at = WHERE[n]
        width = 2 * half

        def lower():
            return jnp.concatenate(
                [sets[which][h * 32:(h + 1) * 32, :, at:at + half].reshape(256, half) for h in range(2)], axis=1
            )

        @pl.when(j == n // 2)
        def _():
            weight[n % 2 * 256:(n % 2 + 1) * 256, 0:width] = lower()

        @pl.when(j >= 2)
        def _():
            part_of = split(lower())
            solved = times(part_of, split(top[0:n + 1].reshape(width, 512)), ((1,), (0,)))
            weight[:, 0:width] = weight[:, 0:width] - times(split(solved), part_of, ((0,), (0,)))

    def arrive(n):
        @pl.when(core == 1)
        def _():
            links.landed(core_slots[n], sets[n], (r - 1, j))

        for m in ((0, 1, 2), (3,))[n]:
            weigh(m)

    do = functools.partial
    plan = {
        0: [event_far],
        1: [do(second_forward, 0), do(bulk_some, BULK[3])],
        3: [do(second_forward, 3)],
        4: [event_share],
        5: [do(leave, 0), do(second_forward, 1), do(over_z, 0), do(bulk_some, BULK[4])],
        6: [do(over_x, 0)],
        7: [do(leave, 1), do(over_y, 0), do(over_z, 1), do(second_forward, 2), do(over_x, 1)],
    }

    def step(k, _):
        @pl.when(is_root & (k == 3))
        def _():
            root_corner()

        @pl.when(is_root)
        def _():
            factor_step(square, inverse, k)

        for n, events in plan.items():
            @pl.when(k == n)
            def _(events=events):
                for event in events:
                    event()

        return 0

    event_pair()

    @pl.when(is_root)
    def _():
        root_square()

    event_near()
    bulk_some(BULK[2])
    lax.fori_loop(0, 8, step, 0)
    event_share_across()
    bulk_some(BULK[5])
    over_core(0)
    over_y(1)
    event_share_end()
    arrive(0)
    over_core(1)
    arrive(1)
    out = pltpu.make_async_copy(weight, wt_ref, local_sem.at[1])
    out.start()
    for o in OFFSETS[1:]:
        second_end(o)
    own_bulk.wait()
    links.landed(bulk_slot, bulk_ref.at[partners[0]], (partners[0], j))
    for n, m, slot in bulk_all:
        links.landed(slot, bulk_ref.at[partners[n], :, pl.ds(512 * m, 512)], (partners[n], j))
    links.drain()
    panel_sends(lambda copy: copy.wait_send())
    pivot_sends(lambda copy: copy.wait_send())

    @pl.when(home)
    def _():
        for copy in share_copies():
            copy.wait_send()

    @pl.when(across)
    def _():
        share_core().wait_send()

    for n in range(2):
        part_sends(n, lambda copy: copy.wait_send())
        for level in range(3):
            level_copies(n, level, lambda copy: copy.wait_send())

        @pl.when(core == 0)
        def _(n=n):
            core_copy(n).wait_send()

    out.wait()


def exchange(maps, live, parent, updates):
    hbm = pl.BlockSpec(memory_space=pl.ANY)
    smem = pl.BlockSpec(memory_space=pltpu.SMEM)
    f32 = jnp.float32
    return pl.pallas_call(
        exchange_body,
        out_shape=(
            jax.ShapeDtypeStruct((8, 4, 256, 512), f32),
            jax.ShapeDtypeStruct((4, 256, 2048), f32),
            jax.ShapeDtypeStruct((512, 1024), f32),
        ),
        in_specs=[smem, smem, hbm, hbm],
        out_specs=(hbm, hbm, hbm),
        scratch_shapes=[
            pltpu.VMEM((4, 256, 256), f32),
            pltpu.VMEM((4, 256, 256), f32),
            pltpu.VMEM((256, 512), f32),
            pltpu.VMEM((4, 256, 512), f32),
            pltpu.VMEM((1024, 1024), f32),
            pltpu.VMEM((512, 512), f32),
            pltpu.VMEM((128, 128), f32),
            pltpu.VMEM((512, 1024), f32),
            *[pltpu.VMEM((64, 8, width), f32) for width in WIDTHS],
            pltpu.SemaphoreType.DMA((SLOTS,)),
            pltpu.SemaphoreType.DMA((SLOTS,)),
            pltpu.SemaphoreType.DMA((3,)),
            pltpu.SemaphoreType.DMA((2, 64)),
            pltpu.SemaphoreType.DMA((2,)),
        ],
        compiler_params=pltpu.CompilerParams(has_side_effects=True, vmem_limit_bytes=40 * 2**20),
    )(maps, live, parent, updates)


def per_device(parent, updates, maps, live):
    panel, bulk, wt = exchange(maps, live, parent, updates)
    place = jnp.stack([lax.axis_index("child"), lax.axis_index("col")]).astype(jnp.int32)
    return finish(place, maps, live, parent, bulk, panel.reshape(8, 1024, 512), wt)


def solution(mesh):
    in_specs = (P("child", "col"), P("child", "col", None), P(), P())
    return jax.shard_map(
        per_device, mesh=mesh, in_specs=in_specs, out_specs=P("child", "col"), check_vma=False
    )
```

time: 268 us -> 234 us (0.87)
  Pallas kernels: 261 us -> 229 us
    pallas_call x1, Pallas kernels: 237 us -> 205 us  [exchange(): pl.pallas_call(exchange_body, out_shape=(jax.ShapeDtypeStruct((8, 4, 256,...]
where the time goes in v2:
time: 234 us
  Pallas kernels  229 us (98%)
  local copies, waits for them, and re-layouts  4.59 us (2%)
    pallas_call x1, Pallas kernels, exchange(): pl.pallas_call(exchange_body, out_shape=(jax.ShapeDtypeStruct((8, 4, 256,...  205 us
    pallas_call x1, Pallas kernels, finish(): pl.pallas_call(finish_body, grid_spec=spec, out_shape=jax.ShapeDtypeStruc...  23.9 us

profile of v2, /device:TPU:37, one launch (start us, length us, event | category | flops | bytes accessed | tf_op | source)
XLA Modules:
  0.0 233.9 jit_solution(2215269444609784834)
XLA Ops:
  0.0 0.1 pad_add_fusion.place_ref
  0.1 0.0 copy-start
  0.1 0.7 copy-done
  0.8 0.0 copy-start.2
  0.8 0.7 copy-done.2
  1.4 0.0 copy-start.1
  1.4 0.0 copy-start.3
  1.4 205.4 %shard_map.46 = (f32[8,4,256,512]{3,2,1,0:T(8,128)}, f32[4,256,2048]{2,1,0:T(8,128)S(1)}, f32[512,1024]{1,0:T(8,128)S(1)}) custom-call(s32[4,64]{1,0:T(4,128)S(1)} %copy-done, s32[4,64]{1,0:T(4,128)S(1)} %copy-done.2, f32[4096,512]{1,0:T(8,128)} %parent_ref.3, f32[1,256,8192]{2,1,0:T(8,128)} %upd_ref.1), custom_call_target="tpu_custom_call" | custom-call | tf_op jit(solution)/shard_map/pallas_call | solution.py:690
  206.8 0.0 copy-start.4
  206.9 3.2 %copy-done.4 = f32[4,256,2048]{2,1,0:T(8,128)} copy-done((f32[4,256,2048]{2,1,0:T(8,128)}, f32[4,256,2048]{2,1,0:T(8,128)S(1)}, u32[]{:S(2)}) %copy-start.4) | copy-done | bytes 8388632
  210.1 0.0 copy-done.1
  210.1 0.0 copy-done.3
  210.1 23.9 %shard_map.47 = f32[4096,512]{1,0:T(8,128)} custom-call(s32[2]{0:T(128)S(1)} %pad_add_fusion.place_ref, s32[4,64]{1,0:T(4,128)S(1)} %copy-done.1, s32[4,64]{1,0:T(4,128)S(1)} %copy-done.3, f32[4096,512]{1,0:T(8,128)} %parent_ref.3, f32[4,256,2048]{2,1,0:T(8,128)} %copy-done.4, f32[8,1024,512]{2,1,0:T(8,128)} %bitcast.3, f32[512,1024]{1,0:T(8,128)S(1)} %get-tuple-element.10.wt_ref), custom_call_target="tpu_custom_call" | custom-call | flops 12884901888 | bytes 47185920 | tf_op jit(solution)/shard_map/pallas_call | solution.py:133
Async XLA Ops:
  0.1 0.7 copy-start
  0.8 0.7 copy-start.2
  1.4 208.6 %copy-start.1 = (s32[4,64]{1,0:T(4,128)S(1)}, s32[4,64]{1,0:T(4,128)}, u32[]{:S(2)}) copy-start(s32[4,64]{1,0:T(4,128)} %map_ref.3) | copy-start | bytes 3076
  1.4 208.6 %copy-start.3 = (s32[4,64]{1,0:T(4,128)S(1)}, s32[4,64]{1,0:T(4,128)}, u32[]{:S(2)}) copy-start(s32[4,64]{1,0:T(4,128)} %live_ref.3) | copy-start | bytes 3076
  206.8 3.2 %copy-start.4 = (f32[4,256,2048]{2,1,0:T(8,128)}, f32[4,256,2048]{2,1,0:T(8,128)S(1)}, u32[]{:S(2)}) copy-start(f32[4,256,2048]{2,1,0:T(8,128)S(1)} %get-tuple-element.8.upd_ref) | copy-start | bytes 25165828

commit v3 on v2

--- a/solution.py
+++ b/solution.py
@@ -101,12 +101,8 @@
         h=w.astype(jnp.bfloat16)
         whi[...]=h
         wlo[...]=(w-h.astype(jnp.float32)).astype(jnp.bfloat16)
-    a=panel_ref[0]
-    ahi=a.astype(jnp.bfloat16)
-    alo=(a-ahi.astype(jnp.float32)).astype(jnp.bfloat16)
-    dot=lambda x,y: jnp.dot(x,y,preferred_element_type=jnp.float32)
-    acc[...]=dot(whi[...],ahi)+(dot(whi[...],alo)+dot(wlo[...],ahi))
     keep=jnp.where(j>=2,1.0,0.0).astype(jnp.float32)
+    acc[...]=jnp.zeros((512,512),jnp.float32)
     for c in range(4):
         for q in range(2):
             col=2*j+q
@@ -118,10 +114,16 @@
                 w=lq*live_ref[c,row].astype(jnp.float32)
                 dst=(pl.ds(pl.multiple_of(bq*128,128),128),pl.ds(pl.multiple_of(ap*128,128),128))
                 acc[dst]=acc[dst]+w*upd_ref[c,q*128:q*128+128,p*128:p*128+128]
-    total=acc[...].T+keep*parent_ref[...]
-    g=r*4096+i*512+lax.broadcasted_iota(jnp.int32,(512,512),0)
-    s=j*512+lax.broadcasted_iota(jnp.int32,(512,512),1)
-    out_ref[...]=jnp.where(g<jnp.minimum(s,1024),0.0,total)
+    dot=lambda x,y: jnp.dot(x,y,preferred_element_type=jnp.float32)
+    for h in range(0,512,512):
+        a=panel_ref[0,:,h:h+512]
+        ahi=a.astype(jnp.bfloat16)
+        alo=(a-ahi.astype(jnp.float32)).astype(jnp.bfloat16)
+        product=dot(whi[...],ahi)+(dot(whi[...],alo)+dot(wlo[...],ahi))
+        total=(product+acc[:,h:h+512]).T+keep*parent_ref[h:h+512,:]
+        g=r*4096+i*512+h+lax.broadcasted_iota(jnp.int32,(512,512),0)
+        s=j*512+lax.broadcasted_iota(jnp.int32,(512,512),1)
+        out_ref[h:h+512,:]=jnp.where(g<jnp.minimum(s,1024),0.0,total)
 def finish(place,maps,live,parent,upd,panel,wt):
     spec=pltpu.PrefetchScalarGridSpec(num_scalar_prefetch=3,grid=(8,),
       in_specs=[pl.BlockSpec((512,512),lambda i,*_:(i,0)),
@@ -634,12 +636,12 @@
         return 0
 
     event_pair()
+    event_near()
 
     @pl.when(is_root)
     def _():
         root_square()
 
-    event_near()
     bulk_some(BULK[2])
     lax.fori_loop(0, 8, step, 0)
     event_share_across()

time: 234 us -> 234 us (level)
  no operation moved by 1% of the time
where the time goes in v3:
time: 234 us; the launch traced here: 233 us
  Pallas kernels  229 us (98%)
  local copies, waits for them, and re-layouts  4.59 us (2%)
    pallas_call x1, Pallas kernels, exchange(): pl.pallas_call(exchange_body, out_shape=(jax.ShapeDtypeStruct((8, 4, 256,...  205 us
    pallas_call x1, Pallas kernels, finish(): pl.pallas_call(finish_body, grid_spec=spec, out_shape=jax.ShapeDtypeStruc...  23.3 us

profile of v3, /device:TPU:37, one launch (start us, length us, event | category | flops | bytes accessed | tf_op | source)
XLA Modules:
  0.0 233.4 jit_solution(16652867849428751178)
XLA Ops:
  0.0 0.1 pad_add_fusion.place_ref
  0.1 0.0 copy-start
  0.1 0.7 copy-done
  0.8 0.0 copy-start.2
  0.8 0.7 copy-done.2
  1.4 0.0 copy-start.1
  1.4 0.0 copy-start.3
  1.4 205.4 %shard_map.46 = (f32[8,4,256,512]{3,2,1,0:T(8,128)}, f32[4,256,2048]{2,1,0:T(8,128)S(1)}, f32[512,1024]{1,0:T(8,128)S(1)}) custom-call(s32[4,64]{1,0:T(4,128)S(1)} %copy-done, s32[4,64]{1,0:T(4,128)S(1)} %copy-done.2, f32[4096,512]{1,0:T(8,128)} %parent_ref.3, f32[1,256,8192]{2,1,0:T(8,128)} %upd_ref.1), custom_call_target="tpu_custom_call" | custom-call | tf_op jit(solution)/shard_map/pallas_call | solution.py:692
  206.8 0.0 copy-start.4
  206.9 3.2 %copy-done.4 = f32[4,256,2048]{2,1,0:T(8,128)} copy-done((f32[4,256,2048]{2,1,0:T(8,128)}, f32[4,256,2048]{2,1,0:T(8,128)S(1)}, u32[]{:S(2)}) %copy-start.4) | copy-done | bytes 8388632
  210.1 0.0 copy-done.1
  210.1 0.0 copy-done.3
  210.1 23.3 %shard_map.47 = f32[4096,512]{1,0:T(8,128)} custom-call(s32[2]{0:T(128)S(1)} %pad_add_fusion.place_ref, s32[4,64]{1,0:T(4,128)S(1)} %copy-done.1, s32[4,64]{1,0:T(4,128)S(1)} %copy-done.3, f32[4096,512]{1,0:T(8,128)} %parent_ref.3, f32[4,256,2048]{2,1,0:T(8,128)} %copy-done.4, f32[8,1024,512]{2,1,0:T(8,128)} %bitcast.3, f32[512,1024]{1,0:T(8,128)S(1)} %get-tuple-element.10.wt_ref), custom_call_target="tpu_custom_call" | custom-call | flops 12884901888 | bytes 47185920 | tf_op jit(solution)/shard_map/pallas_call | solution.py:135
Async XLA Ops:
  0.1 0.7 copy-start
  0.8 0.7 copy-start.2
  1.4 208.6 %copy-start.1 = (s32[4,64]{1,0:T(4,128)S(1)}, s32[4,64]{1,0:T(4,128)}, u32[]{:S(2)}) copy-start(s32[4,64]{1,0:T(4,128)} %map_ref.3) | copy-start | bytes 3076
  1.4 208.6 %copy-start.3 = (s32[4,64]{1,0:T(4,128)S(1)}, s32[4,64]{1,0:T(4,128)}, u32[]{:S(2)}) copy-start(s32[4,64]{1,0:T(4,128)} %live_ref.3) | copy-start | bytes 3076
  206.8 3.2 %copy-start.4 = (f32[4,256,2048]{2,1,0:T(8,128)}, f32[4,256,2048]{2,1,0:T(8,128)S(1)}, u32[]{:S(2)}) copy-start(f32[4,256,2048]{2,1,0:T(8,128)S(1)} %get-tuple-element.8.upd_ref) | copy-start | bytes 25165828
